TPU v7x, 128 devices: a whole 4x4x4 slice. The times are simulated.
128 devices in a mesh: replica: 4 (over z), fsdp: 32 (over y, x, core).
Axes of the slice: x: 4, y: 4, z: 4, core: 2. Of those that a mesh axis runs over, the one named last changes fastest.
Arguments:
- tokens: bfloat16 [4, 16384, 8192], P('replica', 'fsdp'), may hold values from -6 to 6
- next_weights: bfloat16 [4, 8192, 2048], P('replica', 'fsdp'), may hold values from -0.0625 to 0.0625
- inner_weights: bfloat16 [4, 2, 8192, 2048], P('replica', None, 'fsdp'), as said below
- global_weights: float32 [2, 8192, 2048], P(None, 'fsdp', 'replica'), as said below
- momentum: float32 [2, 8192, 2048], P(None, 'fsdp', 'replica'), may hold values from -2 to 2
Outputs:
- projected: bfloat16 [4, 16384, 2048], P('replica', 'fsdp')
- new_global: float32 [2, 8192, 2048], P(None, 'fsdp', 'replica')
- new_momentum: float32 [2, 8192, 2048], P(None, 'fsdp', 'replica')
- normalized: bfloat16 [2, 8192, 2048], P(None, 'fsdp', 'replica')
- mixed_inner: bfloat16 [4, 2, 8192, 2048], P('replica', None, 'fsdp')
- amax: float32 [2, 2], replicated
Inputs may be any that keep to these rules, and one draw needn't show every extreme that they name: `inner_weights`: entries of order a tenth; each replica's inner weights differ from the outer copy by a drift of a fraction of the entry's scale. `global_weights`: entries of order a tenth.
All inputs are finite; a program needn't handle non-finite values.
Results may differ from a plain program's by a relative error of at most 0.015.
Values may be sent and summed in bfloat16 or wider, within the bound.
A program may use at most 128 MiB of HBM per device.

v0:
```python
import jax
import jax.numpy as jnp
from jax import lax
from jax.sharding import PartitionSpec as P

KVW = 1024


outer_rate = 0.7
outer_mom = 0.9
mix_share = 0.5


def on_device(tokens, next_weights, inner_weights, global_weights, momentum):
    tok_rows = tokens[0]
    next_local = next_weights[0]

    def add_rows(piece):
        return jnp.dot(tok_rows, piece, preferred_element_type=jnp.float32)

    key_part = add_rows(lax.all_gather(next_local[:, :KVW], "fsdp", axis=0, tiled=True))
    value_part = add_rows(lax.all_gather(next_local[:, KVW:], "fsdp", axis=0, tiled=True))
    proj_full = jnp.concatenate([key_part, value_part], axis=1)
    projected = proj_full.astype(jnp.bfloat16)[None]
    inner_local = inner_weights[0]
    inner_sum = lax.psum_scatter(inner_local, "replica", scatter_dimension=2, tiled=True).astype(
        jnp.float32
    )
    pseudo = global_weights - inner_sum / lax.axis_size("replica")
    new_momentum = outer_mom * momentum + pseudo
    new_global = global_weights - outer_rate * (pseudo + outer_mom * new_momentum)
    quarter = new_global.shape[2]
    col_index = lax.axis_index("replica") * quarter + jnp.arange(quarter, dtype=jnp.int32)
    key_cols = (col_index < KVW)[None, None, :]
    magnitude = jnp.abs(new_global)
    key_max = jnp.max(jnp.where(key_cols, magnitude, 0.0), axis=(1, 2))
    value_max = jnp.max(jnp.where(key_cols, 0.0, magnitude), axis=(1, 2))
    local_max = jnp.stack([key_max, value_max], axis=1)
    rounded_global = new_global.astype(jnp.bfloat16)
    full_global = lax.all_gather(rounded_global, "replica", axis=2, tiled=True)
    amax = lax.pmax(local_max, ("replica", "fsdp"))
    per_column = jnp.where(key_cols, amax[:, 0][:, None, None], amax[:, 1][:, None, None])
    normalized = (new_global / (per_column + 1e-06)).astype(jnp.bfloat16)
    mixed = mix_share * inner_local.astype(jnp.float32) + (1.0 - mix_share) * full_global.astype(
        jnp.float32
    )
    mixed_inner = mixed.astype(jnp.bfloat16)[None]
    return (projected, new_global, new_momentum, normalized, mixed_inner, amax)


def solution(mesh):
    placed = (
        P("replica", "fsdp", None),
        P("replica", "fsdp", None),
        P("replica", None, "fsdp", None),
        P(None, "fsdp", "replica"),
        P(None, "fsdp", "replica"),
    )
    return jax.shard_map(
        on_device,
        mesh=mesh,
        in_specs=placed,
        out_specs=(
            P("replica", "fsdp", None),
            P(None, "fsdp", "replica"),
            P(None, "fsdp", "replica"),
            P(None, "fsdp", "replica"),
            P("replica", None, "fsdp", None),
            P(),
        ),
        check_vma=False,
    )
```

profile of v0, /device:TPU:1, one launch (start us, length us, event | category | flops | bytes accessed | tf_op | source)
XLA Modules:
  0.0 250.9 jit_solution(9417874637383325405)
XLA Ops:
  7.2 0.0 reduce-scatter.2.cloned.1.call-start
  7.2 0.7 reduce-scatter.2.cloned.1.call-update
  7.9 0.0 all-gather.8.cloned.1.call-start
  7.9 35.6 %reduce-scatter.2.cloned.1.call-done = bf16[2,256,512]{2,1,0:T(8,128)(2,1)} async-done(((bf16[2,256,2048]{2,1,0:T(8,128)(2,1)}), bf16[2,256,512]{2,1,0:T(8,128)(2,1)}) %reduce-scatter.2.cloned.1.call-update) | async-done | bytes 524304 | tf_op jit(solution)/shard_map/reduce_scatter | solution.py:26
  43.6 3.2 %fusion.17 = (bf16[2,256,512]{2,1,0:T(8,128)(2,1)}, f32[2,256,512]{2,1,0:T(8,128)S(1)}, f32[2,256,512]{2,1,0:T(8,128)}) fusion(f32[2,256,512]{2,1,0:T(8,128)} %param.8, bf16[2,256,512]{2,1,0:T(8,128)(2,1)} %reduce-scatter.2.cloned.1.call-done, f32[2,256,512]{2,1,0:T(8,128)} %param.9), kind=kLoop, calls=%fused_computation.22 | loop fusion | flops 2621440 | bytes 5242880 | tf_op jit(solution)/shard_map/convert_element_type | solution.py:39
  46.8 0.0 all-gather.8.cloned.1.call-update
  46.9 0.0 all-gather.6.cloned.1.call-start
  46.9 2.7 %fusion.18 = (bf16[256,1024]{1,0:T(8,128)(2,1)}, bf16[256,1024]{1,0:T(8,128)(2,1)}) fusion(bf16[256,2048]{1,0:T(8,128)(2,1)} %bitcast.31), kind=kLoop, calls=%fused_computation.23 | loop fusion | bytes 2097152 | tf_op jit(solution)/shard_map/slice | solution.py:21
  49.6 0.0 all-gather.6.cloned.1.call-update
  49.6 0.0 all-gather.4.cloned.1.call-start
  49.7 0.5 all-gather.4.cloned.1.call-update
  50.2 0.4 select_reduce_fusion.1
  50.6 65.5 %pmax.7 = f32[2,2]{0,1:T(2,128)S(1)} all-reduce(f32[2,2]{0,1:T(2,128)S(1)} %pad_maximum_fusion.1), channel_id=1, replica_groups=mesh['replica'=4,'fsdp'=32] {'replica','fsdp'}, use_global_device_ids=true, to_apply=%region_3.4 | all-reduce | flops 4 | bytes 32 | tf_op jit(solution)/shard_map/pmax | solution.py:41
  116.1 0.6 copy.11
  116.8 0.1 select_add_fusion
  116.8 0.9 divide_convert_fusion
  117.7 0.0 copy-done.1
  117.7 3.8 %fusion.4 = bf16[1,2,256,2048]{3,2,1,0:T(8,128)(2,1)} fusion(bf16[2,256,2048]{2,1,0:T(8,128)(2,1)} %all-gather.8.cloned.1.call-done, bf16[1,2,256,2048]{3,2,1,0:T(8,128)(2,1)S(1)} %copy-done.1), kind=kLoop, calls=%fused_computation.5 | loop fusion | flops 5242880 | bytes 6291456 | tf_op jit(solution)/shard_map/broadcast_in_dim | solution.py:47
  121.6 0.0 copy-done
  121.6 31.6 %all-gather.6.cloned.1.call-done = bf16[8192,1024]{1,0:T(8,128)(2,1)} async-done(((bf16[256,1024]{1,0:T(8,128)(2,1)}), bf16[8192,1024]{1,0:T(8,128)(2,1)}) %all-gather.6.cloned.1.call-update) | async-done | bytes 16777232 | tf_op jit(solution)/shard_map/all_gather | solution.py:22
  153.2 14.8 %fusion.11 = bf16[1,512,1024]{2,1,0:T(8,128)(2,1)S(1)} fusion(bf16[8192,1024]{1,0:T(8,128)(2,1)} %all-gather.6.cloned.1.call-done, bf16[1,512,8192]{2,1,0:T(8,128)(2,1)} %param.5), kind=kOutput, calls=%fused_computation.9 | convolution fusion | flops 8590458880 | bytes 26214400 | tf_op jit(solution)/shard_map/dot_general | solution.py:19
  168.0 60.1 %all-gather.4.cloned.1.call-done = bf16[8192,1024]{1,0:T(8,128)(2,1)} async-done(((bf16[256,1024]{1,0:T(8,128)(2,1)}), bf16[8192,1024]{1,0:T(8,128)(2,1)}) %all-gather.4.cloned.1.call-update) | async-done | bytes 16777232 | tf_op jit(solution)/shard_map/all_gather | solution.py:21
  228.0 14.8 %fusion.14 = bf16[1,512,1024]{2,1,0:T(8,128)(2,1)S(1)} fusion(bf16[8192,1024]{1,0:T(8,128)(2,1)} %all-gather.4.cloned.1.call-done, bf16[1,512,8192]{2,1,0:T(8,128)(2,1)} %param.5), kind=kOutput, calls=%fused_computation.10 | convolution fusion | flops 8590458880 | bytes 26214400 | tf_op jit(solution)/shard_map/dot_general | solution.py:19
  242.8 1.5 pad_maximum_fusion
  (6 shorter events, 0.0 us)
Async XLA Ops:
  7.2 36.4 %reduce-scatter.2.cloned.1.call-start = ((), (), s32[]{:S(2)}) async-start(), calls=%async_computation.3 | async-start | bytes 2621440 | tf_op jit(solution)/shard_map/reduce_scatter | solution.py:26
  7.9 109.8 %all-gather.8.cloned.1.call-start = ((), (), s32[]{:S(2)}) async-start(), calls=%async_computation.4 | async-start | bytes 2621440 | tf_op jit(solution)/shard_map/all_gather | solution.py:40
  46.8 74.7 %copy-start = (f32[2,256,512]{2,1,0:T(8,128)}, f32[2,256,512]{2,1,0:T(8,128)S(1)}, u32[]{:S(2)}) copy-start(f32[2,256,512]{2,1,0:T(8,128)S(1)} %get-tuple-element.15) | copy-start | bytes 3145732
  46.8 70.9 %copy-start.1 = (bf16[1,2,256,2048]{3,2,1,0:T(8,128)(2,1)S(1)}, bf16[1,2,256,2048]{3,2,1,0:T(8,128)(2,1)}, u32[]{:S(2)}) copy-start(bf16[1,2,256,2048]{3,2,1,0:T(8,128)(2,1)} %param.7) | copy-start | bytes 6291460
  46.9 106.3 %all-gather.6.cloned.1.call-start = ((), (), s32[]{:S(2)}) async-start(), calls=%async_computation.2 | async-start | bytes 17301504 | tf_op jit(solution)/shard_map/all_gather | solution.py:22
  49.6 178.4 %all-gather.4.cloned.1.call-start = ((), (), s32[]{:S(2)}) async-start(), calls=%async_computation.1 | async-start | bytes 17301504 | tf_op jit(solution)/shard_map/all_gather | solution.py:21
Sparse Core Ops, SparseCore 0:
  10.4 33.1 reduce-scatter.1
  47.0 31.4 all-gather.7
  81.0 72.0 all-gather.5
  156.1 71.8 all-gather.3
where the time goes:
time: 251 us
  waiting for transfers between devices  129 us (51%)
  blocking collectives  65.5 us (26%)
  matrix products  29.5 us (12%)
  between operations  13.8 us (5%)
  other arithmetic  9.93 us (4%)
  local copies, waits for them, and re-layouts  3.32 us (1%)
    pmax x1, blocking collectives, on_device(): amax = lax.pmax(local_max, ('replica', 'fsdp'))  65.5 us
    all_gather x1, waiting for transfers between devices, on_device(): lax.all_gather(next_local[:, :KVW], 'fsdp', axis=0, tiled=True)  60.1 us
    reduce_scatter x1, waiting for transfers between devices, on_device(): lax.psum_scatter(inner_local, 'replica', scatter_dimension=2, tiled=True)  35.6 us
    all_gather x1, waiting for transfers between devices, on_device(): lax.all_gather(next_local[:, KVW:], 'fsdp', axis=0, tiled=True)  31.6 us
    dot_general x2, matrix products, add_rows(): return jnp.dot(tok_rows, piece, preferred_element_type=jnp.float32)  29.5 us
  transfers between devices with their start and end apart: 4, of which 3 were waited for; matrix products, arithmetic and copies ran while one was open for 9% of the time, Pallas kernels for 0%

commit v1 on v0

v1 whole, which is shorter than its diff:
```python
import functools

import jax
import jax.numpy as jnp
from jax import lax
from jax.experimental import pallas as pl
from jax.experimental.pallas import tpu as pltpu
from jax.sharding import PartitionSpec as P

MESH = pl.DeviceIdType.MESH
KVW = 1024
SIDE = 4
REPLICAS = 4
DEPTH = 256
QUART = 256
ROWS = 512
COLS = 512
STEPS = 15
CHUNK = 512
outer_rate = 0.7
outer_mom = 0.9
mix_share = 0.5


def build_queues():
    def place(axis, along, across):
        return (along, across) if axis == 0 else (across, along)

    queues = {}
    for axis in (0, 1):
        first = (0, 1) if axis == 0 else (2, 3)
        late = (2, 3) if axis == 0 else (0, 1)
        for sign in (1, -1):
            via, other = (first, late) if sign == 1 else (first[::-1], late[::-1])
            items = [(via[0], 0, 0), (via[1], 0, 0), (via[0],) + place(axis, -sign, 0)]
            items += [(other[0], 0, 0), (other[1], 0, 0)]
            for quarter in other:
                items += [(quarter,) + place(axis, 0, across) for across in (-1, 1, 2)]
            items += [(other[0],) + place(axis, -sign, across) for across in (0, -1, 1, 2)]
            queues[axis, sign] = items
    return queues


QUEUES = build_queues()
WAYS = ((0, 1), (0, -1), (1, 1), (1, -1))


def arrivals(step):
    found = []
    for axis, sign in WAYS:
        quarter, ox, oy = QUEUES[axis, sign][step]
        found.append((quarter, ox - sign, oy) if axis == 0 else (quarter, ox, oy - sign))
    return [(quarter, ox % SIDE, oy % SIDE) for quarter, ox, oy in found]


def token_order():
    order = [(0, 0)]
    for step in range(STEPS):
        for _, ox, oy in arrivals(step):
            if (ox, oy) not in order:
                order.append((ox, oy))
    return order


ORDER = token_order()


def kernel(
    tokens,
    weights,
    inner,
    outer_in,
    momentum_in,
    projected,
    new_global,
    new_momentum,
    normalized,
    mixed,
    amax_out,
    tok,
    wts,
    acc,
    out_stage,
    inner_v,
    parts,
    outer_v,
    momentum_v,
    full,
    peaks,
    ring_send,
    ring_recv,
    tok_here,
    tok_send,
    tok_recv,
    wts_here,
    wts_send,
    wts_recv,
    sum_send,
    sum_recv,
    full_send,
    full_recv,
    peak_send,
    peak_recv,
    out_send,
    out_recv,
    local_sem,
):
    rep = lax.axis_index("replica")
    fsdp = lax.axis_index("fsdp")
    core = fsdp % 2
    x = (fsdp // 2) % SIDE
    y = fsdp // (2 * SIDE)

    def chip_at(ox, oy):
        return ((y + oy) % SIDE) * SIDE + (x + ox) % SIDE

    def at_plane(ox, oy):
        return {"replica": rep, "fsdp": chip_at(ox, oy) * 2 + core}

    def at_replica(oz):
        return {"replica": (rep + oz) % REPLICAS, "fsdp": fsdp}

    sibling = {"replica": rep, "fsdp": chip_at(0, 0) * 2 + 1 - core}
    me = chip_at(0, 0)

    def remote(src, dst, send, recv, device):
        return pltpu.make_async_remote_copy(
            src_ref=src, dst_ref=dst, send_sem=send, recv_sem=recv, device_id=device, device_id_type=MESH
        )

    my_rows = pl.ds(pl.multiple_of(core * ROWS, ROWS), ROWS)
    my_depth = pl.ds(pl.multiple_of(core * DEPTH, DEPTH), DEPTH)

    def columns(which, quarter):
        return pl.ds(pl.multiple_of(which * KVW + quarter * QUART, QUART), QUART)

    locals_ = []

    def start_local(src, dst, sem):
        copy = pltpu.make_async_copy(src, dst, sem)
        copy.start()
        return copy

    w_here = [
        start_local(weights.at[0, :, columns(core, q)], wts.at[me, q, my_depth, :], wts_here.at[q]) for q in range(4)
    ]

    barrier = pltpu.get_barrier_semaphore()
    peers = [sibling] + [at_plane(o, 0) for o in (1, 2, 3)] + [at_plane(0, o) for o in (1, 2, 3)]
    peers += [at_replica(o) for o in (1, 2, 3)]
    for peer in peers:
        pl.semaphore_signal(barrier, inc=1, device_id=peer, device_id_type=MESH)
    pl.semaphore_wait(barrier, len(peers))

    w_far = []
    for q in range(4):
        copy = remote(
            weights.at[0, :, columns(1 - core, q)], wts.at[me, q, my_depth, :], wts_send.at[q], wts_recv.at[q], sibling
        )
        copy.start()
        w_far.append(copy)

    sums = []
    for oz in (1, 2, 3):
        target = (rep + oz) % REPLICAS
        copy = remote(
            inner.at[0, :, :, pl.ds(pl.multiple_of(target * COLS, COLS), COLS)],
            parts.at[rep],
            sum_send.at[oz - 1],
            sum_recv.at[oz - 1],
            at_replica(oz),
        )
        copy.start()
        sums.append(copy)

    def ring_copy(way, step):
        axis, sign = WAYS[way]
        quarter, ox, oy = QUEUES[axis, sign][step]
        block = wts.at[chip_at(ox, oy), quarter]
        device = at_plane(sign, 0) if axis == 0 else at_plane(0, sign)
        return remote(block, block, ring_send.at[way, step], ring_recv.at[way, step], device)

    for q in range(4):
        w_here[q].wait()
        w_far[q].wait_recv()
    ring = {}
    for step in (0, 1):
        for way in range(4):
            ring[way, step] = ring_copy(way, step)
            ring[way, step].start()

    tok_copies = {}
    for n, (ox, oy) in enumerate(ORDER):
        chip = chip_at(ox, oy)
        src = tokens.at[0, :, pl.ds(pl.multiple_of(chip * 2 * DEPTH, 2 * DEPTH), 2 * DEPTH)]
        dst = tok.at[chip, my_rows, :]
        here = start_local(src, dst, tok_here.at[n])
        far = remote(src, dst, tok_send.at[n], tok_recv.at[n], sibling)
        far.start()
        tok_copies[ox, oy] = (here, far)

    own_cols = pl.ds(pl.multiple_of(rep * COLS, COLS), COLS)
    outer_copies = [
        start_local(outer_in, outer_v, local_sem.at[0]),
        start_local(momentum_in, momentum_v, local_sem.at[1]),
        start_local(inner.at[0, :, :, own_cols], parts.at[rep], local_sem.at[2]),
        start_local(inner.at[0], inner_v, local_sem.at[3]),
    ]

    have = set()

    def need_tokens(spots):
        for spot in spots:
            if spot not in have:
                have.add(spot)
                here, far = tok_copies[spot]
                here.wait()
                far.wait_recv()

    def pick(i, values):
        result = values[0]
        for n in range(1, len(values)):
            result = jnp.where(i == n, values[n], result)
        return result

    chunks = 2 * ROWS // CHUNK

    def multiply(items, first):
        need_tokens([(ox, oy) for _, ox, oy in items])
        chips = [chip_at(ox, oy) for _, ox, oy in items]
        quarters = [q for q, _, _ in items]

        def body(i, carry):
            n, m = i // chunks, i % chunks
            chip, quarter = pick(n, chips), pick(n, quarters)
            rows = pl.ds(pl.multiple_of(m * CHUNK, CHUNK), CHUNK)
            part = jnp.dot(tok[chip, rows, :], wts[chip, quarter], preferred_element_type=jnp.float32)
            if first:
                acc[quarter, rows, :] = part
            else:
                acc[quarter, rows, :] += part
            return carry

        lax.fori_loop(0, len(items) * chunks, body, 0)

    LINES = 32
    is_value = rep // 2

    def update():
        for copy in outer_copies[:3]:
            copy.wait()
        for copy in sums:
            copy.wait_recv()
        highest = []
        for layer in range(2):

            def body(i, carry, layer=layer):
                rows = pl.ds(pl.multiple_of(i * LINES, LINES), LINES)
                total = parts[0, layer, rows, :].astype(jnp.float32)
                for r in range(1, REPLICAS):
                    total += parts[r, layer, rows, :].astype(jnp.float32)
                outer = outer_v[layer, rows, :]
                pseudo = outer - total / REPLICAS
                moved = outer_mom * momentum_v[layer, rows, :] + pseudo
                stepped = outer - outer_rate * (pseudo + outer_mom * moved)
                new_momentum[layer, rows, :] = moved
                new_global[layer, rows, :] = stepped
                full[rep, layer, rows, :] = stepped.astype(jnp.bfloat16)
                return jnp.maximum(carry, jnp.abs(stepped))

            top = lax.fori_loop(0, DEPTH // LINES, body, jnp.zeros((LINES, COLS), jnp.float32))
            highest.append(jnp.max(jnp.max(top, axis=0, keepdims=True), axis=1, keepdims=True))
        line = lax.broadcasted_iota(jnp.int32, (8, 128), 0)
        tile = jnp.where(
            line == is_value, highest[0], jnp.where(line == 2 + is_value, highest[1], jnp.zeros((8, 128), jnp.float32))
        )
        copies = []
        for oz in (1, 2, 3):
            copy = remote(
                full.at[rep], full.at[rep], full_send.at[oz - 1], full_recv.at[oz - 1], at_replica(oz)
            )
            copy.start()
            copies.append(copy)
        return tile, copies

    def send_peaks(stage, tile):
        peaks[stage, 0] = tile
        if stage == 3:
            devices = [sibling]
        else:
            devices = [(at_replica(o), at_plane(0, o), at_plane(o, 0))[stage] for o in (1, 2, 3)]
        copies = []
        for n, device in enumerate(devices):
            copy = remote(
                peaks.at[stage, 0], peaks.at[stage, n + 1], peak_send.at[stage, n], peak_recv.at[stage, n], device
            )
            copy.start()
            copies.append(copy)
        return copies

    def take_peaks(stage, copies):
        for copy in copies:
            copy.wait_recv()
        tile = peaks[stage, 0]
        for n in range(len(copies)):
            tile = jnp.maximum(tile, peaks[stage, n + 1])
        return tile

    def normalize(tile):
        values = [[tile[2 * l + t : 2 * l + t + 1, 0:1] for t in range(2)] for l in range(2)]
        row = lax.broadcasted_iota(jnp.int32, (2, 2), 0)
        col = lax.broadcasted_iota(jnp.int32, (2, 2), 1)
        amax_out[...] = jnp.where(
            row == 0,
            jnp.where(col == 0, values[0][0], values[0][1]),
            jnp.where(col == 0, values[1][0], values[1][1]),
        )
        for layer in range(2):
            scale = jnp.where(is_value == 0, values[layer][0], values[layer][1]) + 1e-06

            def body(i, carry, layer=layer, scale=scale):
                rows = pl.ds(pl.multiple_of(i * LINES, LINES), LINES)
                normalized[layer, rows, :] = (new_global[layer, rows, :] / scale).astype(jnp.bfloat16)
                return carry

            lax.fori_loop(0, DEPTH // LINES, body, 0)

    def mix(copies):
        outer_copies[3].wait()
        for copy in copies:
            copy.wait_recv()

        def body(i, carry):
            layer, n = i // (DEPTH // LINES), i % (DEPTH // LINES)
            rows = pl.ds(pl.multiple_of(n * LINES, LINES), LINES)
            for r in range(REPLICAS):
                cols = slice(r * COLS, (r + 1) * COLS)
                value = mix_share * inner_v[layer, rows, cols].astype(jnp.float32)
                value += (1.0 - mix_share) * full[r, layer, rows, :].astype(jnp.float32)
                mixed[0, layer, rows, cols] = value.astype(jnp.bfloat16)
            return carry

        lax.fori_loop(0, 2 * DEPTH // LINES, body, 0)

    multiply([(q, 0, 0) for q in range(4)], True)
    peak_copies = {}
    full_copies = None
    for step in range(STEPS):
        for way in range(4):
            ring[way, step].wait_recv()
        for way in range(4):
            if step + 2 < STEPS:
                ring[way, step].wait_send()
                ring[way, step + 2] = ring_copy(way, step + 2)
                ring[way, step + 2].start()
        if step < STEPS - 1:
            multiply(arrivals(step), False)
        if step == 5:
            tile, full_copies = update()
            peak_copies[0] = send_peaks(0, tile)
        if step in (6, 7, 8):
            tile = take_peaks(step - 6, peak_copies[step - 6])
            peak_copies[step - 5] = send_peaks(step - 5, tile)
        if step == 9:
            tile = take_peaks(3, peak_copies[3])
            normalize(tile)
        if step == 11:
            mix(full_copies)

    last = arrivals(STEPS - 1)
    need_tokens([(ox, oy) for _, ox, oy in last])
    out_copies = []
    other_rows = pl.ds(pl.multiple_of((1 - core) * ROWS, ROWS), ROWS)
    for q, ox, oy in last:
        chip = chip_at(ox, oy)
        part = jnp.dot(tok[chip, other_rows, :], wts[chip, q], preferred_element_type=jnp.float32)
        out_stage[q] = (acc[q, other_rows, :] + part).astype(jnp.bfloat16)
        copy = remote(out_stage.at[q], projected.at[0, :, columns(core, q)], out_send.at[q], out_recv.at[q], sibling)
        copy.start()
        out_copies.append(copy)
    for q, ox, oy in last:
        chip = chip_at(ox, oy)
        part = jnp.dot(tok[chip, my_rows, :], wts[chip, q], preferred_element_type=jnp.float32)
        projected[0, :, columns(core, q)] = (acc[q, my_rows, :] + part).astype(jnp.bfloat16)

    for way in range(4):
        for step in (STEPS - 2, STEPS - 1):
            ring[way, step].wait_send()
    for copy in w_far + sums + full_copies + [far for _, far in tok_copies.values()]:
        copy.wait_send()
    for copies in peak_copies.values():
        for copy in copies:
            copy.wait_send()
    for copy in out_copies:
        copy.wait()


def on_device(tokens, next_weights, inner_weights, global_weights, momentum):
    bf16, f32 = jnp.bfloat16, jnp.float32
    dma = pltpu.SemaphoreType.DMA
    any_ = pl.BlockSpec(memory_space=pl.ANY)
    vmem = pl.BlockSpec(memory_space=pltpu.VMEM)
    layers, depth, wide = inner_weights.shape[1:]
    return pl.pallas_call(
        kernel,
        name="project_and_outer_step",
        out_shape=(
            jax.ShapeDtypeStruct((1, ROWS, 2 * KVW), bf16),
            jax.ShapeDtypeStruct((layers, depth, COLS), f32),
            jax.ShapeDtypeStruct((layers, depth, COLS), f32),
            jax.ShapeDtypeStruct((layers, depth, COLS), bf16),
            jax.ShapeDtypeStruct((1, layers, depth, wide), bf16),
            jax.ShapeDtypeStruct((2, 2), f32),
        ),
        in_specs=[any_] * 5,
        out_specs=(vmem,) * 6,
        scratch_shapes=[
            pltpu.VMEM((SIDE * SIDE, 2 * ROWS, 2 * DEPTH), bf16),
            pltpu.VMEM((SIDE * SIDE, 4, 2 * DEPTH, QUART), bf16),
            pltpu.VMEM((4, 2 * ROWS, QUART), f32),
            pltpu.VMEM((4, ROWS, QUART), bf16),
            pltpu.VMEM((layers, depth, wide), bf16),
            pltpu.VMEM((REPLICAS, layers, depth, COLS), bf16),
            pltpu.VMEM((layers, depth, COLS), f32),
            pltpu.VMEM((layers, depth, COLS), f32),
            pltpu.VMEM((REPLICAS, layers, depth, COLS), bf16),
            pltpu.VMEM((4, 4, 8, 128), f32),
            dma((4, STEPS)),
            dma((4, STEPS)),
            dma((16,)),
            dma((16,)),
            dma((16,)),
            dma((4,)),
            dma((4,)),
            dma((4,)),
            dma((3,)),
            dma((3,)),
            dma((3,)),
            dma((3,)),
            dma((4, 3)),
            dma((4, 3)),
            dma((4,)),
            dma((4,)),
            dma((4,)),
        ],
        compiler_params=pltpu.CompilerParams(
            collective_id=0, has_side_effects=True, vmem_limit_bytes=56 * 1024 * 1024
        ),
    )(tokens, next_weights, inner_weights, global_weights, momentum)


def solution(mesh):
    placed = (
        P("replica", "fsdp", None),
        P("replica", "fsdp", None),
        P("replica", None, "fsdp", None),
        P(None, "fsdp", "replica"),
        P(None, "fsdp", "replica"),
    )
    return jax.shard_map(
        on_device,
        mesh=mesh,
        in_specs=placed,
        out_specs=(
            P("replica", "fsdp", None),
            P(None, "fsdp", "replica"),
            P(None, "fsdp", "replica"),
            P(None, "fsdp", "replica"),
            P("replica", None, "fsdp", None),
            P(),
        ),
        check_vma=False,
    )
```

time: 251 us -> 128 us (0.51)
  waiting for transfers between devices: 129 us -> 0 us
  Pallas kernels: 0 us -> 119 us
  blocking collectives: 65.5 us -> 0 us
  matrix products: 29.5 us -> 0 us
  between operations: 13.8 us -> 0.66 us
  other arithmetic: 9.93 us -> 0 us
  local copies, waits for them, and re-layouts: 3.32 us -> 8.78 us
    pallas_call x0 -> x1, Pallas kernels: none -> 119 us  [on_device(): pl.pallas_call(kernel, name='project_and_outer_step', out_shape=(jax.Shap...]
    all_gather x3 -> x0, waiting for transfers between devices: 91.7 us -> none  [the longest x1 60.1 us: on_device(): lax.all_gather(next_local[:, :KVW], 'fsdp', axis=0, tiled=True)]
    pmax x1 -> x0, blocking collectives: 65.5 us -> none  [on_device(): amax = lax.pmax(local_max, ('replica', 'fsdp'))]
    reduce_scatter x1 -> x0, waiting for transfers between devices: 35.6 us -> none  [on_device(): lax.psum_scatter(inner_local, 'replica', scatter_dimension=2, tiled=True)]
    dot_general x2 -> x0, matrix products: 29.5 us -> none  [add_rows(): return jnp.dot(tok_rows, piece, preferred_element_type=jnp.float32)]
    unnamed x5 -> x16, local copies, waits for them, and re-layouts: 0.65 us -> 8.78 us
    convert_element_type x2 -> x0, other arithmetic: 4.16 us -> none  [the longest x1 3.24 us: on_device(): rounded_global = new_global.astype(jnp.bfloat16)]
    broadcast_in_dim x1 -> x0, other arithmetic: 3.8 us -> none  [on_device(): mixed_inner = mixed.astype(jnp.bfloat16)[None]]
  transfers between devices with their start and end apart: 4 -> 0, of which waited for: 3 -> 0; matrix products, arithmetic and copies ran while one was open for 9% -> 0% of each run, Pallas kernels for 0% -> 0%
where the time goes in v1:
time: 128 us
  Pallas kernels  119 us (93%)
  local copies, waits for them, and re-layouts  8.78 us (7%)
    pallas_call x1, Pallas kernels, on_device(): pl.pallas_call(kernel, name='project_and_outer_step', out_shape=(jax.Shap...  119 us
    unnamed x16, local copies, waits for them, and re-layouts  8.78 us

profile of v1, /device:TPU:1, one launch (start us, length us, event | category | flops | bytes accessed | tf_op | source)
XLA Modules:
  0.0 128.2 jit_solution(8750708479444738588)
XLA Ops:
  0.6 118.7 %project_and_outer_step.1 = (bf16[1,512,2048]{2,1,0:T(8,128)(2,1)}, f32[2,256,512]{2,1,0:T(8,128)}, f32[2,256,512]{2,1,0:T(8,128)}, bf16[2,256,512]{2,1,0:T(8,12...) custom-call(bf16[1,512,8192]{2,1,0:T(8,128)(2,1)} %tokens.1, bf16[1,256,2048]{2,1,0:T(8,128)(2,1)} %weights.1, ...), custom_call_target="tpu_custom_call" | custom-call | tf_op jit(solution)/shard_map/project_and_outer_step/pallas_call | solution.py:404
  119.4 0.0 copy-start.2
  119.4 3.2 %copy.17 = bf16[1,512,2048]{2,1,0:T(8,128)(2,1)} copy(bf16[1,512,2048]{2,1,0:T(8,128)(2,1)} %get-tuple-element.12) | data formatting | bytes 4194304
  122.6 0.0 copy-done.2
  122.6 0.0 copy-start.1
  122.7 0.0 copy-start.3
  122.7 1.0 copy.18
  123.6 0.6 copy-done.1
  124.3 0.0 copy-start
  124.3 1.0 copy.19
  125.2 0.0 copy-done.3
  125.2 0.8 copy.20
  126.0 0.3 copy-done
  126.3 0.0 copy-start.4
  126.3 1.3 %copy.21 = bf16[1,2,256,2048]{3,2,1,0:T(8,128)(2,1)} copy(bf16[1,2,256,2048]{3,2,1,0:T(8,128)(2,1)S(1)} %copy-done) | data formatting | bytes 4194304
  127.6 0.0 copy-done.4
  127.6 0.6 copy.22
Async XLA Ops:
  119.4 3.3 %copy-start.2 = (f32[2,256,512]{2,1,0:T(8,128)S(1)}, f32[2,256,512]{2,1,0:T(8,128)}, u32[]{:S(2)}) copy-start(f32[2,256,512]{2,1,0:T(8,128)} %get-tuple-element.13) | copy-start | bytes 3145732
  122.6 1.6 %copy-start.1 = (f32[2,256,512]{2,1,0:T(8,128)S(1)}, f32[2,256,512]{2,1,0:T(8,128)}, u32[]{:S(2)}) copy-start(f32[2,256,512]{2,1,0:T(8,128)} %get-tuple-element.14) | copy-start | bytes 3145732
  122.7 2.6 %copy-start.3 = (bf16[2,256,512]{2,1,0:T(8,128)(2,1)S(1)}, bf16[2,256,512]{2,1,0:T(8,128)(2,1)}, u32[]{:S(2)}) copy-start(bf16[2,256,512]{2,1,0:T(8,128)(2,1)} %get-tuple-element.15) | copy-start | bytes 1572868
  124.3 2.0 %copy-start = (bf16[1,2,256,2048]{3,2,1,0:T(8,128)(2,1)S(1)}, bf16[1,2,256,2048]{3,2,1,0:T(8,128)(2,1)}, u32[]{:S(2)}) copy-start(bf16[1,2,256,2048]{3,2,1,0:T(8,128)(2,1)} %get-tuple-element.16) | copy-start | bytes 6291460
  126.3 1.3 %copy-start.4 = (f32[2,2]{1,0:T(2,128)S(1)}, f32[2,2]{1,0:T(2,128)}, u32[]{:S(2)}) copy-start(f32[2,2]{1,0:T(2,128)} %get-tuple-element.17) | copy-start | bytes 52

commit v2 on v1

--- a/solution.py
+++ b/solution.py
@@ -16,6 +16,7 @@
 ROWS = 512
 COLS = 512
 STEPS = 15
+AHEAD = 3
 CHUNK = 512
 outer_rate = 0.7
 outer_mom = 0.9
@@ -32,10 +33,10 @@
         late = (2, 3) if axis == 0 else (0, 1)
         for sign in (1, -1):
             via, other = (first, late) if sign == 1 else (first[::-1], late[::-1])
-            items = [(via[0], 0, 0), (via[1], 0, 0), (via[0],) + place(axis, -sign, 0)]
-            items += [(other[0], 0, 0), (other[1], 0, 0)]
-            for quarter in other:
-                items += [(quarter,) + place(axis, 0, across) for across in (-1, 1, 2)]
+            items = [(via[0], 0, 0), (via[1], 0, 0), (other[0], 0, 0), (other[1], 0, 0)]
+            items += [(via[0],) + place(axis, -sign, 0)]
+            items += [(quarter,) + place(axis, 0, across) for quarter in other for across in (-1, 1)]
+            items += [(quarter,) + place(axis, 0, 2) for quarter in other]
             items += [(other[0],) + place(axis, -sign, across) for across in (0, -1, 1, 2)]
             queues[axis, sign] = items
     return queues
@@ -134,8 +135,6 @@
     def columns(which, quarter):
         return pl.ds(pl.multiple_of(which * KVW + quarter * QUART, QUART), QUART)
 
-    locals_ = []
-
     def start_local(src, dst, sem):
         copy = pltpu.make_async_copy(src, dst, sem)
         copy.start()
@@ -159,6 +158,27 @@
         )
         copy.start()
         w_far.append(copy)
+
+    def ring_copy(way, step):
+        axis, sign = WAYS[way]
+        quarter, ox, oy = QUEUES[axis, sign][step]
+        device = at_plane(sign, 0) if axis == 0 else at_plane(0, sign)
+        block = wts.at[chip_at(ox, oy), quarter]
+        if step > 1:
+            return [remote(block, block, ring_send.at[way, step], ring_recv.at[way, step], device)]
+        copies = []
+        for half, which in enumerate((core, 1 - core)):
+            part = wts.at[me, quarter, pl.ds(pl.multiple_of(which * DEPTH, DEPTH), DEPTH), :]
+            slot = step if half == 0 else STEPS + step
+            copies.append(remote(part, part, ring_send.at[way, slot], ring_recv.at[way, slot], device))
+        return copies
+
+    ring = {(way, step): ring_copy(way, step) for way in range(4) for step in range(AHEAD)}
+    for copy in w_here:
+        copy.wait()
+    for step in (0, 1):
+        for way in range(4):
+            ring[way, step][0].start()
 
     sums = []
     for oz in (1, 2, 3):
@@ -173,21 +193,11 @@
         copy.start()
         sums.append(copy)
 
-    def ring_copy(way, step):
-        axis, sign = WAYS[way]
-        quarter, ox, oy = QUEUES[axis, sign][step]
-        block = wts.at[chip_at(ox, oy), quarter]
-        device = at_plane(sign, 0) if axis == 0 else at_plane(0, sign)
-        return remote(block, block, ring_send.at[way, step], ring_recv.at[way, step], device)
-
-    for q in range(4):
-        w_here[q].wait()
-        w_far[q].wait_recv()
-    ring = {}
-    for step in (0, 1):
+    for copy in w_far:
+        copy.wait_recv()
+    for step in range(AHEAD):
         for way in range(4):
-            ring[way, step] = ring_copy(way, step)
-            ring[way, step].start()
+            ring[way, step][-1].start()
 
     tok_copies = {}
     for n, (ox, oy) in enumerate(ORDER):
@@ -274,6 +284,7 @@
         tile = jnp.where(
             line == is_value, highest[0], jnp.where(line == 2 + is_value, highest[1], jnp.zeros((8, 128), jnp.float32))
         )
+        peak_copies[0] = send_peaks(0, tile)
         copies = []
         for oz in (1, 2, 3):
             copy = remote(
@@ -281,7 +292,7 @@
             )
             copy.start()
             copies.append(copy)
-        return tile, copies
+        return copies
 
     def send_peaks(stage, tile):
         peaks[stage, 0] = tile
@@ -344,27 +355,28 @@
 
     multiply([(q, 0, 0) for q in range(4)], True)
     peak_copies = {}
-    full_copies = None
+    full_copies = []
     for step in range(STEPS):
         for way in range(4):
-            ring[way, step].wait_recv()
-        for way in range(4):
-            if step + 2 < STEPS:
-                ring[way, step].wait_send()
-                ring[way, step + 2] = ring_copy(way, step + 2)
-                ring[way, step + 2].start()
+            for copy in ring[way, step]:
+                copy.wait_recv()
+        if step + AHEAD < STEPS:
+            for way in range(4):
+                for copy in ring[way, step]:
+                    copy.wait_send()
+                ring[way, step + AHEAD] = ring_copy(way, step + AHEAD)
+                ring[way, step + AHEAD][0].start()
         if step < STEPS - 1:
             multiply(arrivals(step), False)
-        if step == 5:
-            tile, full_copies = update()
-            peak_copies[0] = send_peaks(0, tile)
-        if step in (6, 7, 8):
-            tile = take_peaks(step - 6, peak_copies[step - 6])
-            peak_copies[step - 5] = send_peaks(step - 5, tile)
-        if step == 9:
-            tile = take_peaks(3, peak_copies[3])
-            normalize(tile)
+        if step == 4:
+            full_copies = update()
+        if step in (6, 8, 10):
+            stage = step // 2 - 3
+            tile = take_peaks(stage, peak_copies[stage])
+            peak_copies[stage + 1] = send_peaks(stage + 1, tile)
         if step == 11:
+            normalize(take_peaks(3, peak_copies[3]))
+        if step == 12:
             mix(full_copies)
 
     last = arrivals(STEPS - 1)
@@ -384,8 +396,8 @@
         projected[0, :, columns(core, q)] = (acc[q, my_rows, :] + part).astype(jnp.bfloat16)
 
     for way in range(4):
-        for step in (STEPS - 2, STEPS - 1):
-            ring[way, step].wait_send()
+        for step in range(STEPS - AHEAD, STEPS):
+            ring[way, step][0].wait_send()
     for copy in w_far + sums + full_copies + [far for _, far in tok_copies.values()]:
         copy.wait_send()
     for copies in peak_copies.values():
@@ -395,23 +407,34 @@
         copy.wait()
 
 
+def write_out(*refs):
+    n = len(refs) // 2
+    sem = refs[-1]
+    copies = [pltpu.make_async_copy(refs[i], refs[n + i], sem.at[i]) for i in range(n)]
+    for copy in copies:
+        copy.start()
+    for copy in copies:
+        copy.wait()
+
+
 def on_device(tokens, next_weights, inner_weights, global_weights, momentum):
     bf16, f32 = jnp.bfloat16, jnp.float32
     dma = pltpu.SemaphoreType.DMA
     any_ = pl.BlockSpec(memory_space=pl.ANY)
     vmem = pl.BlockSpec(memory_space=pltpu.VMEM)
     layers, depth, wide = inner_weights.shape[1:]
-    return pl.pallas_call(
+    results = (
+        ((1, ROWS, 2 * KVW), bf16),
+        ((layers, depth, COLS), f32),
+        ((layers, depth, COLS), f32),
+        ((layers, depth, COLS), bf16),
+        ((1, layers, depth, wide), bf16),
+        ((2, 2), f32),
+    )
+    held = pl.pallas_call(
         kernel,
         name="project_and_outer_step",
-        out_shape=(
-            jax.ShapeDtypeStruct((1, ROWS, 2 * KVW), bf16),
-            jax.ShapeDtypeStruct((layers, depth, COLS), f32),
-            jax.ShapeDtypeStruct((layers, depth, COLS), f32),
-            jax.ShapeDtypeStruct((layers, depth, COLS), bf16),
-            jax.ShapeDtypeStruct((1, layers, depth, wide), bf16),
-            jax.ShapeDtypeStruct((2, 2), f32),
-        ),
+        out_shape=tuple(pltpu.VMEM(*result) for result in results),
         in_specs=[any_] * 5,
         out_specs=(vmem,) * 6,
         scratch_shapes=[
@@ -425,8 +448,8 @@
             pltpu.VMEM((layers, depth, COLS), f32),
             pltpu.VMEM((REPLICAS, layers, depth, COLS), bf16),
             pltpu.VMEM((4, 4, 8, 128), f32),
-            dma((4, STEPS)),
-            dma((4, STEPS)),
+            dma((4, STEPS + 2)),
+            dma((4, STEPS + 2)),
             dma((16,)),
             dma((16,)),
             dma((16,)),
@@ -444,9 +467,19 @@
             dma((4,)),
         ],
         compiler_params=pltpu.CompilerParams(
-            collective_id=0, has_side_effects=True, vmem_limit_bytes=56 * 1024 * 1024
+            collective_id=0, has_side_effects=True, vmem_limit_bytes=52 * 1024 * 1024
         ),
     )(tokens, next_weights, inner_weights, global_weights, momentum)
+    held = [pltpu.with_memory_space_constraint(array, pltpu.VMEM) for array in held]
+    return pl.pallas_call(
+        write_out,
+        name="write_out",
+        out_shape=tuple(jax.ShapeDtypeStruct(*result) for result in results),
+        in_specs=[vmem] * 6,
+        out_specs=(any_,) * 6,
+        scratch_shapes=[dma((6,))],
+        compiler_params=pltpu.CompilerParams(vmem_limit_bytes=8 * 1024 * 1024),
+    )(*held)
 
 
 def solution(mesh):

time: 128 us -> 102 us (0.80)
  Pallas kernels: 119 us -> 101 us
  local copies, waits for them, and re-layouts: 8.78 us -> 0 us
    pallas_call x1 -> x2, Pallas kernels: 119 us -> 101 us  [the longest x1 98.4 us: on_device(): pl.pallas_call(kernel, name='project_and_outer_step', out_shape=tuple((pl...]
    unnamed x16 -> x0, local copies, waits for them, and re-layouts: 8.78 us -> none
where the time goes in v2:
time: 102 us
  Pallas kernels  101 us (99%)
    pallas_call x1, Pallas kernels, on_device(): pl.pallas_call(kernel, name='project_and_outer_step', out_shape=tuple((pl...  98.4 us
    pallas_call x1, Pallas kernels, on_device(): pl.pallas_call(write_out, name='write_out', out_shape=tuple((jax.ShapeDty...  2.91 us

profile of v2, /device:TPU:1, one launch (start us, length us, event | category | flops | bytes accessed | tf_op | source)
XLA Modules:
  0.0 102.0 jit_solution(6417810722120369258)
XLA Ops:
  0.6 98.4 %project_and_outer_step.1 = (bf16[1,512,2048]{2,1,0:T(8,128)(2,1)S(1)}, f32[2,256,512]{2,1,0:T(8,128)S(1)}, f32[2,256,512]{2,1,0:T(8,128)S(1)}, bf16[2,256,512]{...) custom-call(bf16[1,512,8192]{2,1,0:T(8,128)(2,1)} %tokens.1, ...), custom_call_target="tpu_custom_call" | custom-call | tf_op jit(solution)/shard_map/project_and_outer_step/pallas_call | solution.py:434
  99.1 2.9 %write_out.1 = (bf16[1,512,2048]{2,1,0:T(8,128)(2,1)}, f32[2,256,512]{2,1,0:T(8,128)}, f32[2,256,512]{2,1,0:T(8,128)}, bf16[2,256,512]{2,1,0:T(8,128)(2,1)}, bf1...) custom-call(bf16[1,512,2048]{2,1,0:T(8,128)(2,1)S(1)} %get-tuple-element.12.refs_0_, ...), custom_call_target="tpu_custom_call" | custom-call | tf_op jit(solution)/shard_map/write_out/pallas_call | solution.py:474

commit v3 on v2

--- a/solution.py
+++ b/solution.py
@@ -17,6 +17,7 @@
 COLS = 512
 STEPS = 15
 AHEAD = 3
+REUSE = 2 * AHEAD
 CHUNK = 512
 outer_rate = 0.7
 outer_mom = 0.9
@@ -36,8 +37,9 @@
             items = [(via[0], 0, 0), (via[1], 0, 0), (other[0], 0, 0), (other[1], 0, 0)]
             items += [(via[0],) + place(axis, -sign, 0)]
             items += [(quarter,) + place(axis, 0, across) for quarter in other for across in (-1, 1)]
-            items += [(quarter,) + place(axis, 0, 2) for quarter in other]
-            items += [(other[0],) + place(axis, -sign, across) for across in (0, -1, 1, 2)]
+            ends = [(quarter,) + place(axis, 0, 2) for quarter in other]
+            passed = [(other[0],) + place(axis, -sign, across) for across in (0, -1, 1, 2)]
+            items += ends + passed if sign == 1 else ends[:1] + passed + ends[1:]
             queues[axis, sign] = items
     return queues
 
@@ -52,18 +54,6 @@
         quarter, ox, oy = QUEUES[axis, sign][step]
         found.append((quarter, ox - sign, oy) if axis == 0 else (quarter, ox, oy - sign))
     return [(quarter, ox % SIDE, oy % SIDE) for quarter, ox, oy in found]
-
-
-def token_order():
-    order = [(0, 0)]
-    for step in range(STEPS):
-        for _, ox, oy in arrivals(step):
-            if (ox, oy) not in order:
-                order.append((ox, oy))
-    return order
-
-
-ORDER = token_order()
 
 
 def kernel(
@@ -81,11 +71,14 @@
     tok,
     wts,
     acc,
-    out_stage,
+    out_far,
+    out_here,
     inner_v,
     parts,
     outer_v,
     momentum_v,
+    normal_v,
+    amax_v,
     full,
     peaks,
     ring_send,
@@ -105,6 +98,7 @@
     out_send,
     out_recv,
     local_sem,
+    result_sem,
 ):
     rep = lax.axis_index("replica")
     fsdp = lax.axis_index("fsdp")
@@ -145,11 +139,32 @@
     ]
 
     barrier = pltpu.get_barrier_semaphore()
-    peers = [sibling] + [at_plane(o, 0) for o in (1, 2, 3)] + [at_plane(0, o) for o in (1, 2, 3)]
-    peers += [at_replica(o) for o in (1, 2, 3)]
+    peers = [sibling] + [at_plane(o, 0) for o in (1, 3)] + [at_plane(0, o) for o in (1, 3)]
+    peers += [at_replica(o) for o in (1, 3)]
     for peer in peers:
         pl.semaphore_signal(barrier, inc=1, device_id=peer, device_id_type=MESH)
     pl.semaphore_wait(barrier, len(peers))
+
+    def ring_copy(way, step):
+        axis, sign = WAYS[way]
+        quarter, ox, oy = QUEUES[axis, sign][step]
+        device = at_plane(sign, 0) if axis == 0 else at_plane(0, sign)
+        block = wts.at[chip_at(ox, oy), quarter]
+        if step > 1:
+            return [remote(block, block, ring_send.at[way, step % AHEAD], ring_recv.at[way, step % REUSE], device)]
+        copies = []
+        for half, which in enumerate((core, 1 - core)):
+            part = wts.at[me, quarter, pl.ds(pl.multiple_of(which * DEPTH, DEPTH), DEPTH), :]
+            src = weights.at[0, :, columns(core, quarter)] if half == 0 else part
+            send = ring_send.at[way, step if half == 0 else AHEAD + step]
+            recv = ring_recv.at[way, step if half == 0 else REUSE + step]
+            copies.append(remote(src, part, send, recv, device))
+        return copies
+
+    ring = {(way, step): ring_copy(way, step) for way in range(4) for step in range(AHEAD)}
+    for step in (0, 1):
+        for way in range(4):
+            ring[way, step][0].start()
 
     w_far = []
     for q in range(4):
@@ -159,40 +174,22 @@
         copy.start()
         w_far.append(copy)
 
-    def ring_copy(way, step):
-        axis, sign = WAYS[way]
-        quarter, ox, oy = QUEUES[axis, sign][step]
-        device = at_plane(sign, 0) if axis == 0 else at_plane(0, sign)
-        block = wts.at[chip_at(ox, oy), quarter]
-        if step > 1:
-            return [remote(block, block, ring_send.at[way, step], ring_recv.at[way, step], device)]
-        copies = []
-        for half, which in enumerate((core, 1 - core)):
-            part = wts.at[me, quarter, pl.ds(pl.multiple_of(which * DEPTH, DEPTH), DEPTH), :]
-            slot = step if half == 0 else STEPS + step
-            copies.append(remote(part, part, ring_send.at[way, slot], ring_recv.at[way, slot], device))
-        return copies
-
-    ring = {(way, step): ring_copy(way, step) for way in range(4) for step in range(AHEAD)}
-    for copy in w_here:
-        copy.wait()
-    for step in (0, 1):
-        for way in range(4):
-            ring[way, step][0].start()
-
-    sums = []
-    for oz in (1, 2, 3):
+    def sum_copy(oz):
         target = (rep + oz) % REPLICAS
-        copy = remote(
+        return remote(
             inner.at[0, :, :, pl.ds(pl.multiple_of(target * COLS, COLS), COLS)],
             parts.at[rep],
             sum_send.at[oz - 1],
             sum_recv.at[oz - 1],
             at_replica(oz),
         )
-        copy.start()
-        sums.append(copy)
-
+
+    sums = [sum_copy(oz) for oz in (1, 2, 3)]
+    sums[0].start()
+    sums[2].start()
+
+    for copy in w_here:
+        copy.wait()
     for copy in w_far:
         copy.wait_recv()
     for step in range(AHEAD):
@@ -200,14 +197,15 @@
             ring[way, step][-1].start()
 
     tok_copies = {}
-    for n, (ox, oy) in enumerate(ORDER):
-        chip = chip_at(ox, oy)
-        src = tokens.at[0, :, pl.ds(pl.multiple_of(chip * 2 * DEPTH, 2 * DEPTH), 2 * DEPTH)]
-        dst = tok.at[chip, my_rows, :]
+    for n, oy in enumerate((0, 3, 1, 2)):
+        line = (y + oy) % SIDE
+        width = SIDE * 2 * DEPTH
+        src = tokens.at[0, :, pl.ds(pl.multiple_of(line * width, width), width)]
+        dst = tok.at[line, my_rows, :]
         here = start_local(src, dst, tok_here.at[n])
         far = remote(src, dst, tok_send.at[n], tok_recv.at[n], sibling)
         far.start()
-        tok_copies[ox, oy] = (here, far)
+        tok_copies[oy] = (here, far)
 
     own_cols = pl.ds(pl.multiple_of(rep * COLS, COLS), COLS)
     outer_copies = [
@@ -235,16 +233,24 @@
 
     chunks = 2 * ROWS // CHUNK
 
+    def product(rows, ox, oy, quarter):
+        cols = pl.ds(pl.multiple_of(ox * 2 * DEPTH, 2 * DEPTH), 2 * DEPTH)
+        return jnp.dot(tok[oy, rows, cols], wts[oy * SIDE + ox, quarter], preferred_element_type=jnp.float32)
+
+    def owner(ox, oy):
+        return (x + ox) % SIDE, (y + oy) % SIDE
+
     def multiply(items, first):
-        need_tokens([(ox, oy) for _, ox, oy in items])
-        chips = [chip_at(ox, oy) for _, ox, oy in items]
+        need_tokens([oy for _, _, oy in items])
         quarters = [q for q, _, _ in items]
+        lines = [owner(ox, oy) for _, ox, oy in items]
 
         def body(i, carry):
             n, m = i // chunks, i % chunks
-            chip, quarter = pick(n, chips), pick(n, quarters)
+            quarter = pick(n, quarters)
+            ox, oy = pick(n, [line[0] for line in lines]), pick(n, [line[1] for line in lines])
             rows = pl.ds(pl.multiple_of(m * CHUNK, CHUNK), CHUNK)
-            part = jnp.dot(tok[chip, rows, :], wts[chip, quarter], preferred_element_type=jnp.float32)
+            part = product(rows, ox, oy, quarter)
             if first:
                 acc[quarter, rows, :] = part
             else:
@@ -253,14 +259,33 @@
 
         lax.fori_loop(0, len(items) * chunks, body, 0)
 
+    other_rows = pl.ds(pl.multiple_of((1 - core) * ROWS, ROWS), ROWS)
+    out_copies = []
+
+    def finish(items):
+        for rows, stage in ((other_rows, out_far), (my_rows, out_here)):
+            for q in items:
+                value = acc[q, rows, :]
+                for ox, oy in items[q]:
+                    value += product(rows, *owner(ox, oy), q)
+                stage[q] = value.astype(jnp.bfloat16)
+                place = projected.at[0, :, columns(core, q)]
+                if stage is out_far:
+                    copy = remote(stage.at[q], place, out_send.at[q], out_recv.at[q], sibling)
+                    copy.start()
+                else:
+                    copy = start_local(stage.at[q], place, result_sem.at[q])
+                out_copies.append(copy)
+
     LINES = 32
     is_value = rep // 2
+
+    results = []
 
     def update():
         for copy in outer_copies[:3]:
             copy.wait()
-        for copy in sums:
-            copy.wait_recv()
+        sums[1].wait_recv()
         highest = []
         for layer in range(2):
 
@@ -273,13 +298,15 @@
                 pseudo = outer - total / REPLICAS
                 moved = outer_mom * momentum_v[layer, rows, :] + pseudo
                 stepped = outer - outer_rate * (pseudo + outer_mom * moved)
-                new_momentum[layer, rows, :] = moved
-                new_global[layer, rows, :] = stepped
+                momentum_v[layer, rows, :] = moved
+                outer_v[layer, rows, :] = stepped
                 full[rep, layer, rows, :] = stepped.astype(jnp.bfloat16)
                 return jnp.maximum(carry, jnp.abs(stepped))
 
             top = lax.fori_loop(0, DEPTH // LINES, body, jnp.zeros((LINES, COLS), jnp.float32))
             highest.append(jnp.max(jnp.max(top, axis=0, keepdims=True), axis=1, keepdims=True))
+        results.append(start_local(momentum_v, new_momentum, result_sem.at[4]))
+        results.append(start_local(outer_v, new_global, result_sem.at[5]))
         line = lax.broadcasted_iota(jnp.int32, (8, 128), 0)
         tile = jnp.where(
             line == is_value, highest[0], jnp.where(line == 2 + is_value, highest[1], jnp.zeros((8, 128), jnp.float32))
@@ -303,7 +330,7 @@
         copies = []
         for n, device in enumerate(devices):
             copy = remote(
-                peaks.at[stage, 0], peaks.at[stage, n + 1], peak_send.at[stage, n], peak_recv.at[stage, n], device
+                peaks.at[stage, 0], peaks.at[stage, n + 1], peak_send.at[n], peak_recv.at[stage, n], device
             )
             copy.start()
             copies.append(copy)
@@ -311,7 +338,7 @@
 
     def take_peaks(stage, copies):
         for copy in copies:
-            copy.wait_recv()
+            copy.wait()
         tile = peaks[stage, 0]
         for n in range(len(copies)):
             tile = jnp.maximum(tile, peaks[stage, n + 1])
@@ -321,7 +348,7 @@
         values = [[tile[2 * l + t : 2 * l + t + 1, 0:1] for t in range(2)] for l in range(2)]
         row = lax.broadcasted_iota(jnp.int32, (2, 2), 0)
         col = lax.broadcasted_iota(jnp.int32, (2, 2), 1)
-        amax_out[...] = jnp.where(
+        amax_v[...] = jnp.where(
             row == 0,
             jnp.where(col == 0, values[0][0], values[0][1]),
             jnp.where(col == 0, values[1][0], values[1][1]),
@@ -331,10 +358,12 @@
 
             def body(i, carry, layer=layer, scale=scale):
                 rows = pl.ds(pl.multiple_of(i * LINES, LINES), LINES)
-                normalized[layer, rows, :] = (new_global[layer, rows, :] / scale).astype(jnp.bfloat16)
+                normal_v[layer, rows, :] = (outer_v[layer, rows, :] / scale).astype(jnp.bfloat16)
                 return carry
 
             lax.fori_loop(0, DEPTH // LINES, body, 0)
+        results.append(start_local(normal_v, normalized, result_sem.at[6]))
+        results.append(start_local(amax_v, amax_out, result_sem.at[7]))
 
     def mix(copies):
         outer_copies[3].wait()
@@ -348,10 +377,11 @@
                 cols = slice(r * COLS, (r + 1) * COLS)
                 value = mix_share * inner_v[layer, rows, cols].astype(jnp.float32)
                 value += (1.0 - mix_share) * full[r, layer, rows, :].astype(jnp.float32)
-                mixed[0, layer, rows, cols] = value.astype(jnp.bfloat16)
+                inner_v[layer, rows, cols] = value.astype(jnp.bfloat16)
             return carry
 
         lax.fori_loop(0, 2 * DEPTH // LINES, body, 0)
+        results.append(start_local(inner_v, mixed.at[0], result_sem.at[8]))
 
     multiply([(q, 0, 0) for q in range(4)], True)
     peak_copies = {}
@@ -368,6 +398,12 @@
                 ring[way, step + AHEAD][0].start()
         if step < STEPS - 1:
             multiply(arrivals(step), False)
+        if step == STEPS - 2:
+            finish({1: [], 3: []})
+        if step == 1:
+            sums[0].wait_recv()
+            sums[2].wait_recv()
+            sums[1].start()
         if step == 4:
             full_copies = update()
         if step in (6, 8, 10):
@@ -379,31 +415,18 @@
         if step == 12:
             mix(full_copies)
 
-    last = arrivals(STEPS - 1)
-    need_tokens([(ox, oy) for _, ox, oy in last])
-    out_copies = []
-    other_rows = pl.ds(pl.multiple_of((1 - core) * ROWS, ROWS), ROWS)
-    for q, ox, oy in last:
-        chip = chip_at(ox, oy)
-        part = jnp.dot(tok[chip, other_rows, :], wts[chip, q], preferred_element_type=jnp.float32)
-        out_stage[q] = (acc[q, other_rows, :] + part).astype(jnp.bfloat16)
-        copy = remote(out_stage.at[q], projected.at[0, :, columns(core, q)], out_send.at[q], out_recv.at[q], sibling)
-        copy.start()
-        out_copies.append(copy)
-    for q, ox, oy in last:
-        chip = chip_at(ox, oy)
-        part = jnp.dot(tok[chip, my_rows, :], wts[chip, q], preferred_element_type=jnp.float32)
-        projected[0, :, columns(core, q)] = (acc[q, my_rows, :] + part).astype(jnp.bfloat16)
+    last = {}
+    for q, ox, oy in arrivals(STEPS - 1):
+        last.setdefault(q, []).append((ox, oy))
+    need_tokens([oy for items in last.values() for _, oy in items])
+    finish(last)
 
     for way in range(4):
         for step in range(STEPS - AHEAD, STEPS):
             ring[way, step][0].wait_send()
     for copy in w_far + sums + full_copies + [far for _, far in tok_copies.values()]:
         copy.wait_send()
-    for copies in peak_copies.values():
-        for copy in copies:
-            copy.wait_send()
-    for copy in out_copies:
+    for copy in out_copies + results:
         copy.wait()
 
 
@@ -421,7 +444,6 @@
     bf16, f32 = jnp.bfloat16, jnp.float32
     dma = pltpu.SemaphoreType.DMA
     any_ = pl.BlockSpec(memory_space=pl.ANY)
-    vmem = pl.BlockSpec(memory_space=pltpu.VMEM)
     layers, depth, wide = inner_weights.shape[1:]
     results = (
         ((1, ROWS, 2 * KVW), bf16),
@@ -436,35 +458,39 @@
         name="project_and_outer_step",
         out_shape=tuple(pltpu.VMEM(*result) for result in results),
         in_specs=[any_] * 5,
-        out_specs=(vmem,) * 6,
+        out_specs=(any_,) * 6,
         scratch_shapes=[
-            pltpu.VMEM((SIDE * SIDE, 2 * ROWS, 2 * DEPTH), bf16),
+            pltpu.VMEM((SIDE, 2 * ROWS, SIDE * 2 * DEPTH), bf16),
             pltpu.VMEM((SIDE * SIDE, 4, 2 * DEPTH, QUART), bf16),
             pltpu.VMEM((4, 2 * ROWS, QUART), f32),
+            pltpu.VMEM((4, ROWS, QUART), bf16),
             pltpu.VMEM((4, ROWS, QUART), bf16),
             pltpu.VMEM((layers, depth, wide), bf16),
             pltpu.VMEM((REPLICAS, layers, depth, COLS), bf16),
             pltpu.VMEM((layers, depth, COLS), f32),
             pltpu.VMEM((layers, depth, COLS), f32),
+            pltpu.VMEM((layers, depth, COLS), bf16),
+            pltpu.VMEM((2, 2), f32),
             pltpu.VMEM((REPLICAS, layers, depth, COLS), bf16),
             pltpu.VMEM((4, 4, 8, 128), f32),
-            dma((4, STEPS + 2)),
-            dma((4, STEPS + 2)),
-            dma((16,)),
-            dma((16,)),
-            dma((16,)),
-            dma((4,)),
-            dma((4,)),
-            dma((4,)),
+            dma((4, AHEAD + 2)),
+            dma((4, REUSE + 2)),
+            dma((4,)),
+            dma((4,)),
+            dma((4,)),
+            dma((4,)),
+            dma((4,)),
+            dma((4,)),
+            dma((3,)),
             dma((3,)),
             dma((3,)),
             dma((3,)),
             dma((3,)),
             dma((4, 3)),
-            dma((4, 3)),
-            dma((4,)),
-            dma((4,)),
-            dma((4,)),
+            dma((4,)),
+            dma((4,)),
+            dma((4,)),
+            dma((9,)),
         ],
         compiler_params=pltpu.CompilerParams(
             collective_id=0, has_side_effects=True, vmem_limit_bytes=52 * 1024 * 1024
@@ -475,7 +501,7 @@
         write_out,
         name="write_out",
         out_shape=tuple(jax.ShapeDtypeStruct(*result) for result in results),
-        in_specs=[vmem] * 6,
+        in_specs=[any_] * 6,
         out_specs=(any_,) * 6,
         scratch_shapes=[dma((6,))],
         compiler_params=pltpu.CompilerParams(vmem_limit_bytes=8 * 1024 * 1024),

time: 102 us -> 101 us (level)
    pallas_call x1, Pallas kernels: 98.4 us -> 97.2 us  [on_device(): pl.pallas_call(kernel, name='project_and_outer_step', out_shape=tuple((pl...]
where the time goes in v3:
time: 101 us
  Pallas kernels  100 us (99%)
    pallas_call x1, Pallas kernels, on_device(): pl.pallas_call(kernel, name='project_and_outer_step', out_shape=tuple((pl...  97.2 us
    pallas_call x1, Pallas kernels, on_device(): pl.pallas_call(write_out, name='write_out', out_shape=tuple((jax.ShapeDty...  2.91 us

profile of v3, /device:TPU:1, one launch (start us, length us, event | category | flops | bytes accessed | tf_op | source)
XLA Modules:
  0.0 100.8 jit_solution(2218696891573647807)
XLA Ops:
  0.6 97.2 %project_and_outer_step.1 = (bf16[1,512,2048]{2,1,0:T(8,128)(2,1)S(1)}, f32[2,256,512]{2,1,0:T(8,128)S(1)}, f32[2,256,512]{2,1,0:T(8,128)S(1)}, bf16[2,256,512]{...) custom-call(bf16[1,512,8192]{2,1,0:T(8,128)(2,1)} %tokens.1, ...), custom_call_target="tpu_custom_call" | custom-call | tf_op jit(solution)/shard_map/project_and_outer_step/pallas_call | solution.py:456
  97.9 2.9 %write_out.1 = (bf16[1,512,2048]{2,1,0:T(8,128)(2,1)}, f32[2,256,512]{2,1,0:T(8,128)}, f32[2,256,512]{2,1,0:T(8,128)}, bf16[2,256,512]{2,1,0:T(8,128)(2,1)}, bf1...) custom-call(bf16[1,512,2048]{2,1,0:T(8,128)(2,1)S(1)} %get-tuple-element.12.refs_0_, ...), custom_call_target="tpu_custom_call" | custom-call | tf_op jit(solution)/shard_map/write_out/pallas_call | solution.py:500

commit v4 on v3

--- a/solution.py
+++ b/solution.py
@@ -71,8 +71,7 @@
     tok,
     wts,
     acc,
-    out_far,
-    out_here,
+    out_stage,
     inner_v,
     parts,
     outer_v,
@@ -99,6 +98,7 @@
     out_recv,
     local_sem,
     result_sem,
+    greet,
 ):
     rep = lax.axis_index("replica")
     fsdp = lax.axis_index("fsdp")
@@ -138,12 +138,32 @@
         start_local(weights.at[0, :, columns(core, q)], wts.at[me, q, my_depth, :], wts_here.at[q]) for q in range(4)
     ]
 
+    def signal(sem, device):
+        pl.semaphore_signal(sem, inc=1, device_id=device, device_id_type=MESH)
+
     barrier = pltpu.get_barrier_semaphore()
-    peers = [sibling] + [at_plane(o, 0) for o in (1, 3)] + [at_plane(0, o) for o in (1, 3)]
-    peers += [at_replica(o) for o in (1, 3)]
-    for peer in peers:
-        pl.semaphore_signal(barrier, inc=1, device_id=peer, device_id_type=MESH)
-    pl.semaphore_wait(barrier, len(peers))
+    plane = [sibling] + [at_plane(o, 0) for o in (1, 3)] + [at_plane(0, o) for o in (1, 3)]
+    for peer in plane:
+        signal(barrier, peer)
+    first, last_rep = rep == 0, rep == REPLICAS - 1
+
+    @pl.when(jnp.logical_not(last_rep))
+    def _():
+        signal(barrier, at_replica(1))
+
+    @pl.when(first)
+    def _():
+        signal(barrier, at_replica(REPLICAS - 1))
+
+    pl.semaphore_wait(barrier, len(plane) + jnp.minimum(rep, 1) + rep // (REPLICAS - 1))
+
+    @pl.when(jnp.logical_not(first))
+    def _():
+        signal(greet, at_replica(REPLICAS - 1))
+
+    @pl.when(last_rep)
+    def _():
+        signal(greet, at_replica(1))
 
     def ring_copy(way, step):
         axis, sign = WAYS[way]
@@ -185,9 +205,6 @@
         )
 
     sums = [sum_copy(oz) for oz in (1, 2, 3)]
-    sums[0].start()
-    sums[2].start()
-
     for copy in w_here:
         copy.wait()
     for copy in w_far:
@@ -214,6 +231,13 @@
         start_local(inner.at[0, :, :, own_cols], parts.at[rep], local_sem.at[2]),
         start_local(inner.at[0], inner_v, local_sem.at[3]),
     ]
+
+    @pl.when(jnp.logical_not(last_rep))
+    def _():
+        pl.semaphore_wait(greet, 2 - jnp.minimum(rep, 1))
+
+    sums[0].start()
+    sums[2].start()
 
     have = set()
 
@@ -259,23 +283,37 @@
 
         lax.fori_loop(0, len(items) * chunks, body, 0)
 
-    other_rows = pl.ds(pl.multiple_of((1 - core) * ROWS, ROWS), ROWS)
-    out_copies = []
+    def out_copy(half, q):
+        place = projected.at[0, :, columns(core, q)]
+        if half == 0:
+            return remote(out_stage.at[0, q], place, out_send.at[q], out_recv.at[q], sibling)
+        return pltpu.make_async_copy(out_stage.at[1, q], place, result_sem.at[q])
 
     def finish(items):
-        for rows, stage in ((other_rows, out_far), (my_rows, out_here)):
-            for q in items:
-                value = acc[q, rows, :]
-                for ox, oy in items[q]:
-                    value += product(rows, *owner(ox, oy), q)
-                stage[q] = value.astype(jnp.bfloat16)
-                place = projected.at[0, :, columns(core, q)]
-                if stage is out_far:
-                    copy = remote(stage.at[q], place, out_send.at[q], out_recv.at[q], sibling)
-                    copy.start()
-                else:
-                    copy = start_local(stage.at[q], place, result_sem.at[q])
-                out_copies.append(copy)
+        quarters = list(items)
+        lines = [[owner(ox, oy) for ox, oy in items[q]] for q in quarters]
+
+        def body(i, carry):
+            half, n = i // len(quarters), i % len(quarters)
+            q = pick(n, quarters)
+            rows = pl.ds(pl.multiple_of(jnp.where(half == 0, 1 - core, core) * ROWS, ROWS), ROWS)
+            value = acc[q, rows, :]
+            for spot in range(len(lines[0])):
+                ox, oy = (pick(n, [line[spot][axis] for line in lines]) for axis in (0, 1))
+                value += product(rows, ox, oy, q)
+            out_stage[half, q] = value.astype(jnp.bfloat16)
+
+            @pl.when(half == 0)
+            def _():
+                out_copy(0, q).start()
+
+            @pl.when(half == 1)
+            def _():
+                out_copy(1, q).start()
+
+            return carry
+
+        lax.fori_loop(0, 2 * len(quarters), body, 0)
 
     LINES = 32
     is_value = rep // 2
@@ -400,17 +438,17 @@
             multiply(arrivals(step), False)
         if step == STEPS - 2:
             finish({1: [], 3: []})
-        if step == 1:
+        if step == 2:
             sums[0].wait_recv()
             sums[2].wait_recv()
             sums[1].start()
-        if step == 4:
+        if step == 5:
             full_copies = update()
-        if step in (6, 8, 10):
-            stage = step // 2 - 3
+        if step in (7, 9, 11):
+            stage = (step - 7) // 2
             tile = take_peaks(stage, peak_copies[stage])
             peak_copies[stage + 1] = send_peaks(stage + 1, tile)
-        if step == 11:
+        if step == 12:
             normalize(take_peaks(3, peak_copies[3]))
         if step == 12:
             mix(full_copies)
@@ -426,7 +464,7 @@
             ring[way, step][0].wait_send()
     for copy in w_far + sums + full_copies + [far for _, far in tok_copies.values()]:
         copy.wait_send()
-    for copy in out_copies + results:
+    for copy in [out_copy(half, q) for half in (0, 1) for q in range(4)] + results:
         copy.wait()
 
 
@@ -463,8 +501,7 @@
             pltpu.VMEM((SIDE, 2 * ROWS, SIDE * 2 * DEPTH), bf16),
             pltpu.VMEM((SIDE * SIDE, 4, 2 * DEPTH, QUART), bf16),
             pltpu.VMEM((4, 2 * ROWS, QUART), f32),
-            pltpu.VMEM((4, ROWS, QUART), bf16),
-            pltpu.VMEM((4, ROWS, QUART), bf16),
+            pltpu.VMEM((2, 4, ROWS, QUART), bf16),
             pltpu.VMEM((layers, depth, wide), bf16),
             pltpu.VMEM((REPLICAS, layers, depth, COLS), bf16),
             pltpu.VMEM((layers, depth, COLS), f32),
@@ -491,6 +528,7 @@
             dma((4,)),
             dma((4,)),
             dma((9,)),
+            pltpu.SemaphoreType.REGULAR,
         ],
         compiler_params=pltpu.CompilerParams(
             collective_id=0, has_side_effects=True, vmem_limit_bytes=52 * 1024 * 1024

time: 101 us -> 99.2 us (0.982)
  Pallas kernels: 100 us -> 98.4 us
    pallas_call x1, Pallas kernels: 97.2 us -> 95.5 us  [on_device(): pl.pallas_call(kernel, name='project_and_outer_step', out_shape=tuple((pl...]
where the time goes in v4:
time: 99.2 us; the launch traced here: 99.1 us
  Pallas kernels  98.4 us (99%)
    pallas_call x1, Pallas kernels, on_device(): pl.pallas_call(kernel, name='project_and_outer_step', out_shape=tuple((pl...  95.5 us
    pallas_call x1, Pallas kernels, on_device(): pl.pallas_call(write_out, name='write_out', out_shape=tuple((jax.ShapeDty...  2.91 us

profile of v4, /device:TPU:1, one launch (start us, length us, event | category | flops | bytes accessed | tf_op | source)
XLA Modules:
  0.0 99.1 jit_solution(6106143054319924322)
XLA Ops:
  0.6 95.5 %project_and_outer_step.1 = (bf16[1,512,2048]{2,1,0:T(8,128)(2,1)S(1)}, f32[2,256,512]{2,1,0:T(8,128)S(1)}, f32[2,256,512]{2,1,0:T(8,128)S(1)}, bf16[2,256,512]{...) custom-call(bf16[1,512,8192]{2,1,0:T(8,128)(2,1)} %tokens.1, ...), custom_call_target="tpu_custom_call" | custom-call | tf_op jit(solution)/shard_map/project_and_outer_step/pallas_call | solution.py:494
  96.1 2.9 %write_out.1 = (bf16[1,512,2048]{2,1,0:T(8,128)(2,1)}, f32[2,256,512]{2,1,0:T(8,128)}, f32[2,256,512]{2,1,0:T(8,128)}, bf16[2,256,512]{2,1,0:T(8,128)(2,1)}, bf1...) custom-call(bf16[1,512,2048]{2,1,0:T(8,128)(2,1)S(1)} %get-tuple-element.12.refs_0_, ...), custom_call_target="tpu_custom_call" | custom-call | tf_op jit(solution)/shard_map/write_out/pallas_call | solution.py:538

commit v5 on v4

--- a/solution.py
+++ b/solution.py
@@ -107,13 +107,13 @@
     y = fsdp // (2 * SIDE)
 
     def chip_at(ox, oy):
-        return ((y + oy) % SIDE) * SIDE + (x + ox) % SIDE
+        return ((y + oy + SIDE) % SIDE) * SIDE + (x + ox + SIDE) % SIDE
 
     def at_plane(ox, oy):
         return {"replica": rep, "fsdp": chip_at(ox, oy) * 2 + core}
 
     def at_replica(oz):
-        return {"replica": (rep + oz) % REPLICAS, "fsdp": fsdp}
+        return {"replica": (rep + oz + REPLICAS) % REPLICAS, "fsdp": fsdp}
 
     sibling = {"replica": rep, "fsdp": chip_at(0, 0) * 2 + 1 - core}
     me = chip_at(0, 0)
@@ -134,36 +134,40 @@
         copy.start()
         return copy
 
-    w_here = [
-        start_local(weights.at[0, :, columns(core, q)], wts.at[me, q, my_depth, :], wts_here.at[q]) for q in range(4)
-    ]
-
     def signal(sem, device):
         pl.semaphore_signal(sem, inc=1, device_id=device, device_id_type=MESH)
 
+    axes = ((x, lambda o: at_plane(o, 0)), (y, lambda o: at_plane(0, o)), (rep, at_replica))
     barrier = pltpu.get_barrier_semaphore()
-    plane = [sibling] + [at_plane(o, 0) for o in (1, 3)] + [at_plane(0, o) for o in (1, 3)]
-    for peer in plane:
-        signal(barrier, peer)
-    first, last_rep = rep == 0, rep == REPLICAS - 1
-
-    @pl.when(jnp.logical_not(last_rep))
-    def _():
-        signal(barrier, at_replica(1))
-
-    @pl.when(first)
-    def _():
-        signal(barrier, at_replica(REPLICAS - 1))
-
-    pl.semaphore_wait(barrier, len(plane) + jnp.minimum(rep, 1) + rep // (REPLICAS - 1))
-
-    @pl.when(jnp.logical_not(first))
-    def _():
-        signal(greet, at_replica(REPLICAS - 1))
-
-    @pl.when(last_rep)
-    def _():
-        signal(greet, at_replica(1))
+    for place, at in axes:
+
+        @pl.when(place < SIDE - 1)
+        def _(at=at):
+            signal(barrier, at(1))
+
+        @pl.when(place == 0)
+        def _(at=at):
+            signal(barrier, at(-1))
+
+    signal(barrier, sibling)
+    lower = [jnp.minimum(place, 1) + place // (SIDE - 1) for place, _ in axes]
+    pl.semaphore_wait(barrier, 1 + lower[0] + lower[1] + lower[2])
+    for axis, (place, at) in enumerate(axes):
+
+        @pl.when(place > 0)
+        def _(at=at, axis=axis):
+            signal(greet.at[2 * axis], at(-1))
+
+        @pl.when(place == SIDE - 1)
+        def _(at=at, axis=axis):
+            signal(greet.at[2 * axis + 1], at(1))
+
+    def await_answer(axis, sign):
+        place = axes[axis][0]
+
+        @pl.when(place < SIDE - 1 if sign == 1 else place == 0)
+        def _():
+            pl.semaphore_wait(greet.at[2 * axis + (0 if sign == 1 else 1)], 1)
 
     def ring_copy(way, step):
         axis, sign = WAYS[way]
@@ -182,10 +186,6 @@
         return copies
 
     ring = {(way, step): ring_copy(way, step) for way in range(4) for step in range(AHEAD)}
-    for step in (0, 1):
-        for way in range(4):
-            ring[way, step][0].start()
-
     w_far = []
     for q in range(4):
         copy = remote(
@@ -193,6 +193,24 @@
         )
         copy.start()
         w_far.append(copy)
+
+    def begin(ways):
+        for way in ways:
+            await_answer(*WAYS[way])
+            for step in (0, 1):
+                ring[way, step][0].start()
+
+    @pl.when(x == 0)
+    def _():
+        begin((2, 3, 0, 1))
+
+    @pl.when(x > 0)
+    def _():
+        begin((0, 1, 2, 3))
+
+    w_here = [
+        start_local(weights.at[0, :, columns(core, q)], wts.at[me, q, my_depth, :], wts_here.at[q]) for q in range(4)
+    ]
 
     def sum_copy(oz):
         target = (rep + oz) % REPLICAS
@@ -232,10 +250,8 @@
         start_local(inner.at[0], inner_v, local_sem.at[3]),
     ]
 
-    @pl.when(jnp.logical_not(last_rep))
-    def _():
-        pl.semaphore_wait(greet, 2 - jnp.minimum(rep, 1))
-
+    for sign in (1, -1):
+        await_answer(2, sign)
     sums[0].start()
     sums[2].start()
 
@@ -528,7 +544,7 @@
             dma((4,)),
             dma((4,)),
             dma((9,)),
-            pltpu.SemaphoreType.REGULAR,
+            pltpu.SemaphoreType.REGULAR((6,)),
         ],
         compiler_params=pltpu.CompilerParams(
             collective_id=0, has_side_effects=True, vmem_limit_bytes=52 * 1024 * 1024

time: 99.2 us -> 97.8 us (0.986)
  Pallas kernels: 98.4 us -> 96.7 us
    pallas_call x1, Pallas kernels: 95.5 us -> 93.8 us  [on_device(): pl.pallas_call(kernel, name='project_and_outer_step', out_shape=tuple((pl...]
where the time goes in v5:
time: 97.8 us; the launch traced here: 97.3 us
  Pallas kernels  96.7 us (99%)
    pallas_call x1, Pallas kernels, on_device(): pl.pallas_call(kernel, name='project_and_outer_step', out_shape=tuple((pl...  93.8 us
    pallas_call x1, Pallas kernels, on_device(): pl.pallas_call(write_out, name='write_out', out_shape=tuple((jax.ShapeDty...  2.91 us

profile of v5, /device:TPU:1, one launch (start us, length us, event | category | flops | bytes accessed | tf_op | source)
XLA Modules:
  0.0 97.3 jit_solution(7521702227371380776)
XLA Ops:
  0.6 93.8 %project_and_outer_step.1 = (bf16[1,512,2048]{2,1,0:T(8,128)(2,1)S(1)}, f32[2,256,512]{2,1,0:T(8,128)S(1)}, f32[2,256,512]{2,1,0:T(8,128)S(1)}, bf16[2,256,512]{...) custom-call(bf16[1,512,8192]{2,1,0:T(8,128)(2,1)} %tokens.1, ...), custom_call_target="tpu_custom_call" | custom-call | tf_op jit(solution)/shard_map/project_and_outer_step/pallas_call | solution.py:510
  94.4 2.9 %write_out.1 = (bf16[1,512,2048]{2,1,0:T(8,128)(2,1)}, f32[2,256,512]{2,1,0:T(8,128)}, f32[2,256,512]{2,1,0:T(8,128)}, bf16[2,256,512]{2,1,0:T(8,128)(2,1)}, bf1...) custom-call(bf16[1,512,2048]{2,1,0:T(8,128)(2,1)S(1)} %get-tuple-element.12.refs_0_, ...), custom_call_target="tpu_custom_call" | custom-call | tf_op jit(solution)/shard_map/write_out/pallas_call | solution.py:554

commit v6 on v5

--- a/solution.py
+++ b/solution.py
@@ -16,7 +16,7 @@
 ROWS = 512
 COLS = 512
 STEPS = 15
-AHEAD = 3
+AHEAD = 2
 REUSE = 2 * AHEAD
 CHUNK = 512
 outer_rate = 0.7
@@ -85,18 +85,13 @@
     tok_here,
     tok_send,
     tok_recv,
-    wts_here,
-    wts_send,
-    wts_recv,
     sum_send,
     sum_recv,
-    full_send,
     full_recv,
     peak_send,
     peak_recv,
     out_send,
     out_recv,
-    local_sem,
     result_sem,
     greet,
 ):
@@ -189,7 +184,7 @@
     w_far = []
     for q in range(4):
         copy = remote(
-            weights.at[0, :, columns(1 - core, q)], wts.at[me, q, my_depth, :], wts_send.at[q], wts_recv.at[q], sibling
+            weights.at[0, :, columns(1 - core, q)], wts.at[me, q, my_depth, :], out_send.at[q], out_recv.at[q], sibling
         )
         copy.start()
         w_far.append(copy)
@@ -209,7 +204,7 @@
         begin((0, 1, 2, 3))
 
     w_here = [
-        start_local(weights.at[0, :, columns(core, q)], wts.at[me, q, my_depth, :], wts_here.at[q]) for q in range(4)
+        start_local(weights.at[0, :, columns(core, q)], wts.at[me, q, my_depth, :], result_sem.at[q]) for q in range(4)
     ]
 
     def sum_copy(oz):
@@ -244,10 +239,10 @@
 
     own_cols = pl.ds(pl.multiple_of(rep * COLS, COLS), COLS)
     outer_copies = [
-        start_local(outer_in, outer_v, local_sem.at[0]),
-        start_local(momentum_in, momentum_v, local_sem.at[1]),
-        start_local(inner.at[0, :, :, own_cols], parts.at[rep], local_sem.at[2]),
-        start_local(inner.at[0], inner_v, local_sem.at[3]),
+        start_local(outer_in, outer_v, result_sem.at[4]),
+        start_local(momentum_in, momentum_v, result_sem.at[5]),
+        start_local(inner.at[0, :, :, own_cols], parts.at[rep], result_sem.at[6]),
+        start_local(inner.at[0], inner_v, result_sem.at[8]),
     ]
 
     for sign in (1, -1):
@@ -340,6 +335,8 @@
         for copy in outer_copies[:3]:
             copy.wait()
         sums[1].wait_recv()
+        for copy in sums:
+            copy.wait_send()
         highest = []
         for layer in range(2):
 
@@ -369,7 +366,7 @@
         copies = []
         for oz in (1, 2, 3):
             copy = remote(
-                full.at[rep], full.at[rep], full_send.at[oz - 1], full_recv.at[oz - 1], at_replica(oz)
+                full.at[rep], full.at[rep], sum_send.at[oz - 1], full_recv.at[oz - 1], at_replica(oz)
             )
             copy.start()
             copies.append(copy)
@@ -440,7 +437,7 @@
     multiply([(q, 0, 0) for q in range(4)], True)
     peak_copies = {}
     full_copies = []
-    for step in range(STEPS):
+    for step in range(STEPS - 1):
         for way in range(4):
             for copy in ring[way, step]:
                 copy.wait_recv()
@@ -450,14 +447,15 @@
                     copy.wait_send()
                 ring[way, step + AHEAD] = ring_copy(way, step + AHEAD)
                 ring[way, step + AHEAD][0].start()
-        if step < STEPS - 1:
-            multiply(arrivals(step), False)
+        multiply(arrivals(step), False)
         if step == STEPS - 2:
             finish({1: [], 3: []})
         if step == 2:
             sums[0].wait_recv()
             sums[2].wait_recv()
             sums[1].start()
+            for copy in w_far:
+                copy.wait_send()
         if step == 5:
             full_copies = update()
         if step in (7, 9, 11):
@@ -473,12 +471,26 @@
     for q, ox, oy in arrivals(STEPS - 1):
         last.setdefault(q, []).append((ox, oy))
     need_tokens([oy for items in last.values() for _, oy in items])
-    finish(last)
+
+    def conclude(ways):
+        for pair in ways:
+            for way in pair:
+                ring[way, STEPS - 1][0].wait_recv()
+            q = arrivals(STEPS - 1)[pair[0]][0]
+            finish({q: last[q]})
+
+    @pl.when(x == 0)
+    def _():
+        conclude(((2, 3), (0, 1)))
+
+    @pl.when(x > 0)
+    def _():
+        conclude(((0, 1), (2, 3)))
 
     for way in range(4):
         for step in range(STEPS - AHEAD, STEPS):
             ring[way, step][0].wait_send()
-    for copy in w_far + sums + full_copies + [far for _, far in tok_copies.values()]:
+    for copy in full_copies + [far for _, far in tok_copies.values()]:
         copy.wait_send()
     for copy in [out_copy(half, q) for half in (0, 1) for q in range(4)] + results:
         copy.wait()
@@ -531,16 +543,11 @@
             dma((4,)),
             dma((4,)),
             dma((4,)),
-            dma((4,)),
-            dma((4,)),
-            dma((4,)),
-            dma((3,)),
             dma((3,)),
             dma((3,)),
             dma((3,)),
             dma((3,)),
             dma((4, 3)),
-            dma((4,)),
             dma((4,)),
             dma((4,)),
             dma((9,)),

time: 97.8 us -> 97.7 us (level)
  no operation moved by 1% of the time
where the time goes in v6:
time: 97.7 us; the launch traced here: 97.6 us
  Pallas kernels  96.9 us (99%)
    pallas_call x1, Pallas kernels, on_device(): pl.pallas_call(kernel, name='project_and_outer_step', out_shape=tuple((pl...  94 us
    pallas_call x1, Pallas kernels, on_device(): pl.pallas_call(write_out, name='write_out', out_shape=tuple((jax.ShapeDty...  2.91 us

profile of v6, /device:TPU:1, one launch (start us, length us, event | category | flops | bytes accessed | tf_op | source)
XLA Modules:
  0.0 97.6 jit_solution(510712835469088524)
XLA Ops:
  0.6 94.0 %project_and_outer_step.1 = (bf16[1,512,2048]{2,1,0:T(8,128)(2,1)S(1)}, f32[2,256,512]{2,1,0:T(8,128)S(1)}, f32[2,256,512]{2,1,0:T(8,128)S(1)}, bf16[2,256,512]{...) custom-call(bf16[1,512,8192]{2,1,0:T(8,128)(2,1)} %tokens.1, ...), custom_call_target="tpu_custom_call" | custom-call | tf_op jit(solution)/shard_map/project_and_outer_step/pallas_call | solution.py:522
  94.7 2.9 %write_out.1 = (bf16[1,512,2048]{2,1,0:T(8,128)(2,1)}, f32[2,256,512]{2,1,0:T(8,128)}, f32[2,256,512]{2,1,0:T(8,128)}, bf16[2,256,512]{2,1,0:T(8,128)(2,1)}, bf1...) custom-call(bf16[1,512,2048]{2,1,0:T(8,128)(2,1)S(1)} %get-tuple-element.12.refs_0_, ...), custom_call_target="tpu_custom_call" | custom-call | tf_op jit(solution)/shard_map/write_out/pallas_call | solution.py:561

commit v7 on v6

--- a/solution.py
+++ b/solution.py
@@ -18,7 +18,7 @@
 STEPS = 15
 AHEAD = 2
 REUSE = 2 * AHEAD
-CHUNK = 512
+CHUNK = 1024
 outer_rate = 0.7
 outer_mom = 0.9
 mix_share = 0.5

time: 97.7 us -> 97.7 us (level)
  no operation moved by 1% of the time
where the time goes in v7:
time: 97.7 us; the launch traced here: 97.6 us
  Pallas kernels  96.9 us (99%)
    pallas_call x1, Pallas kernels, on_device(): pl.pallas_call(kernel, name='project_and_outer_step', out_shape=tuple((pl...  94 us
    pallas_call x1, Pallas kernels, on_device(): pl.pallas_call(write_out, name='write_out', out_shape=tuple((jax.ShapeDty...  2.91 us

profile of v7, /device:TPU:1, one launch (start us, length us, event | category | flops | bytes accessed | tf_op | source)
XLA Modules:
  0.0 97.6 jit_solution(10980395817637222442)
XLA Ops:
  0.6 94.0 %project_and_outer_step.1 = (bf16[1,512,2048]{2,1,0:T(8,128)(2,1)S(1)}, f32[2,256,512]{2,1,0:T(8,128)S(1)}, f32[2,256,512]{2,1,0:T(8,128)S(1)}, bf16[2,256,512]{...) custom-call(bf16[1,512,8192]{2,1,0:T(8,128)(2,1)} %tokens.1, ...), custom_call_target="tpu_custom_call" | custom-call | tf_op jit(solution)/shard_map/project_and_outer_step/pallas_call | solution.py:522
  94.7 2.9 %write_out.1 = (bf16[1,512,2048]{2,1,0:T(8,128)(2,1)}, f32[2,256,512]{2,1,0:T(8,128)}, f32[2,256,512]{2,1,0:T(8,128)}, bf16[2,256,512]{2,1,0:T(8,128)(2,1)}, bf1...) custom-call(bf16[1,512,2048]{2,1,0:T(8,128)(2,1)S(1)} %get-tuple-element.12.refs_0_, ...), custom_call_target="tpu_custom_call" | custom-call | tf_op jit(solution)/shard_map/write_out/pallas_call | solution.py:561
